TPU v7x, 512 devices: a whole 4x8x8 slice. The times are simulated.
512 devices in a mesh: bucket: 128 (over x, y, z_lo, core), rep: 4 (over z_hi).
Axes of the slice: x: 4, y: 8, z: 8 (z_hi: 4, z_lo: 2; z = z_hi * 2 + z_lo), core: 2. Of those that a mesh axis runs over, the one named last changes fastest.
Arguments:
- src_table: float32 [262144, 256], P(('bucket', 'rep')), may hold values from -6 to 6
- src_state: float32 [262144], P(('bucket', 'rep')), may hold values from 0.05 to 0.5
- dst_table: float32 [65536, 256], P(('bucket', 'rep')), may hold values from -6 to 6
- dst_state: float32 [65536], P(('bucket', 'rep')), may hold values from 0.05 to 0.5
- rel_table: float32 [64, 256], replicated, may hold values from 0.25 to 1.75
- partners: int32 [2, 128], replicated, may hold values from 0 to 127, as said below
- tiles: int32 [128, 4, 2, 64], P('bucket', 'rep'), may hold values from 0 to 15
- tile_rel: int32 [128, 4, 2, 64], P('bucket', 'rep'), may hold values from 0 to 63
- counts: int32 [128, 4, 2], P('bucket', 'rep'), may hold values from 1 to 64, as said below
Outputs:
- src_out: float32 [262144, 256], P(('bucket', 'rep'))
- src_state_out: float32 [262144], P(('bucket', 'rep'))
- dst_out: float32 [65536, 256], P(('bucket', 'rep'))
- dst_state_out: float32 [65536], P(('bucket', 'rep'))
Inputs may be any that keep to these rules, and one draw needn't show every extreme that they name: partners[k, b] = b XOR m_k for one mask m_k of round k, 1 to 127, a different mask in each round. Only the first counts[b, r, k] slots of a device's round are live; some device holds 64 live tiles in every draw.
All inputs are finite; a program needn't handle non-finite values.
Results may differ from a plain program's by a relative error of at most 0.002.
Values may be sent and summed in bfloat16 or wider, within the bound.
A program may use at most 64 MiB of HBM per device.

v0:
```python
import jax
import jax.numpy as jnp
from jax import lax
from jax.sharding import PartitionSpec as P

D = 256
TILE = 128
TILE_GROUP = 8
ROUNDS = 2
MAXT = 64


learn_rate = 0.1


def partner(array, axis, bit):
    return lax.ppermute(array, axis, [(i, i ^ 1 << bit) for i in range(lax.axis_size(axis))])


def from_everyone(array, axis):
    copies = jnp.broadcast_to(array, (lax.axis_size(axis), *array.shape))
    return lax.all_to_all(copies, axis, split_axis=0, concat_axis=0, tiled=True)


def joined_along(parts, dim):
    dims = list(parts.shape[1:])
    dims[dim] *= parts.shape[0]
    return jnp.moveaxis(parts, 0, dim).reshape(dims)


def gather_directly(array, axis, dim):
    parts = from_everyone(array, axis)
    return joined_along(parts, dim)


def cut_along(array, dim, length):
    dims = array.shape
    parts = array.reshape(*dims[:dim], length, dims[dim] // length, *dims[dim + 1 :])
    return jnp.moveaxis(parts, dim, 0)


def sum_at_owner(array, axis, dim):
    length = lax.axis_size(axis)
    parts = lax.all_to_all(cut_along(array, dim, length), axis, 0, 0, tiled=True)
    return jnp.sum(parts.astype(jnp.float32), axis=0)


def step_bit(moved, rows, round_mask, bit_number):
    flag = jnp.bitwise_and(jnp.right_shift(round_mask, bit_number), 1) == 1
    return lax.cond(flag, moved, lambda values: values, rows)


def route_slice(rows, round_mask, bit_count):
    for bit_number in range(bit_count):

        def moved(values, bit_number=bit_number):
            return partner(values, "bucket", bit_number)

        rows = step_bit(moved, rows, round_mask, bit_number)
    return rows


def return_slice(rows, round_mask, bit_count):
    for bit_number in range(bit_count):

        def moved(values, bit_number=bit_number):
            return partner(values, "bucket", bit_number)

        rows = step_bit(moved, rows, round_mask, bit_number)
    return rows


def tile_work(src_rows, partition, tile_list, rel_list, live_count, rel_table):
    dst_number = partition.shape[0] // TILE
    src_number = src_rows.shape[0] // TILE
    rel_number = rel_table.shape[0]
    score_scale = D ** (-0.5)
    src_blocks = src_rows.reshape(src_number, TILE, D)
    dst_blocks = partition.reshape(dst_number, TILE, D)
    group_count = MAXT // TILE_GROUP
    tile_grid = tile_list.reshape(group_count, TILE_GROUP)
    rel_grid = rel_list.reshape(group_count, TILE_GROUP)
    slot_grid = jnp.arange(MAXT, dtype=jnp.int32).reshape(group_count, TILE_GROUP)
    diagonal_ones = jnp.eye(TILE, dtype=jnp.float32)
    src_range = jnp.arange(src_number, dtype=jnp.int32)
    dst_range = jnp.arange(dst_number, dtype=jnp.int32)
    rel_range = jnp.arange(rel_number, dtype=jnp.int32)

    def group_step(totals, group_item):
        src_total, dst_total = totals
        tile_ids, rel_ids, slot_ids = group_item
        src_index = tile_ids // dst_number
        dst_index = tile_ids % dst_number
        rel_onehot = (rel_ids[:, None] == rel_range[None, :]).astype(jnp.float32)
        rel_pick = jnp.dot(rel_onehot, rel_table)
        src_pick = jnp.take(src_blocks, src_index, axis=0)
        dst_pick = jnp.take(dst_blocks, dst_index, axis=0)
        src_rel = (src_pick * rel_pick[:, None, :]).astype(jnp.bfloat16)
        scores = (
            jnp.einsum("tnd,tmd->tnm", src_rel, dst_pick, preferred_element_type=jnp.float32)
            * score_scale
        )
        live_tiles = (slot_ids < live_count).astype(jnp.float32)
        slope = ((jax.nn.sigmoid(scores) - diagonal_ones) * live_tiles[:, None, None]).astype(
            jnp.bfloat16
        )
        src_terms = (
            jnp.einsum("tnm,tmd->tnd", slope, dst_pick, preferred_element_type=jnp.float32)
            * rel_pick[:, None, :]
            * score_scale
        )
        dst_terms = (
            jnp.einsum("tnm,tnd->tmd", slope, src_rel, preferred_element_type=jnp.float32)
            * score_scale
        )
        src_onehot = (src_index[:, None] == src_range[None, :]).astype(jnp.float32)
        dst_onehot = (dst_index[:, None] == dst_range[None, :]).astype(jnp.float32)
        src_total = src_total + jnp.einsum("ts,tnd->snd", src_onehot, src_terms)
        dst_total = dst_total + jnp.einsum("ts,tnd->snd", dst_onehot, dst_terms)
        return ((src_total, dst_total), None)

    start_totals = (
        jnp.zeros((src_number, TILE, D), jnp.float32),
        jnp.zeros((dst_number, TILE, D), jnp.float32),
    )
    (src_total, dst_total), unused = lax.scan(
        group_step, start_totals, (tile_grid, rel_grid, slot_grid)
    )
    return (src_total.reshape(-1, D), dst_total.reshape(-1, D))


def adagrad(embedding, accumulator, gradient):
    accumulator = accumulator + jnp.mean(gradient * gradient, axis=1)
    embedding = embedding - learn_rate * gradient / jnp.sqrt(accumulator)[:, None]
    return (embedding, accumulator)


def per_device(
    src_table, src_state, dst_table, dst_state, rel_table, partners, tiles, tile_rel, counts
):
    bit_count = lax.axis_size("bucket").bit_length() - 1
    for round_index in range(ROUNDS):
        round_mask = partners[round_index, 0]
        own_rows = dst_table.astype(jnp.bfloat16)
        moved_rows = route_slice(own_rows, round_mask, bit_count)
        partition = gather_directly(moved_rows, "rep", 0)
        src_grad, dst_part = tile_work(
            src_table.astype(jnp.bfloat16),
            partition,
            tiles[0, 0, round_index],
            tile_rel[0, 0, round_index],
            counts[0, 0, round_index],
            rel_table,
        )
        summed = sum_at_owner(dst_part.astype(jnp.bfloat16), "rep", 0).astype(jnp.bfloat16)
        dst_grad = return_slice(summed, round_mask, bit_count).astype(jnp.float32)
        src_table, src_state = adagrad(src_table, src_state, src_grad)
        dst_table, dst_state = adagrad(dst_table, dst_state, dst_grad)
    return (src_table, src_state, dst_table, dst_state)


def solution(mesh):
    in_specs = (
        P(("bucket", "rep"), None),
        P(("bucket", "rep")),
        P(("bucket", "rep"), None),
        P(("bucket", "rep")),
        P(),
        P(),
        P("bucket", "rep", None, None),
        P("bucket", "rep", None, None),
        P("bucket", "rep", None),
    )
    out_specs = (
        P(("bucket", "rep"), None),
        P(("bucket", "rep")),
        P(("bucket", "rep"), None),
        P(("bucket", "rep")),
    )
    return jax.shard_map(
        per_device, mesh=mesh, in_specs=in_specs, out_specs=out_specs, check_vma=False
    )
```

profile of v0, /device:TPU:30, one launch (start us, length us, event | category | flops | bytes accessed | tf_op | source)
XLA Modules:
  0.0 263.1 jit_solution(2624311033611704599)
XLA Ops:
  10.5 6.7 %conditional.37 = (bf16[128,256]{1,0:T(8,128)(2,1)S(1)}) conditional(s32[]{:T(128)} %bitcast.6, bf16[128,256]{1,0:T(8,128)(2,1)S(1)} %get-tuple-element.1021, bf16[128,256]{1,0:T(8,128)(2,1)S(1)} %get-tuple-element.1021), branch_computations={%region_2.0_spmd, %region_3.0_spmd} | conditional | bytes 393264 | solution.py:50
  10.5 4.3 %collective-permute-start.1 = (bf16[128,256]{1,0:T(8,128)(2,1)S(1)}, bf16[128,256]{1,0:T(8,128)(2,1)S(1)}, u32[]{:S(2)}, u32[]{:S(2)}) collective-permute-start(bf16[128,256]{1,0:T(8,128)(2,1)S(1)} %param.3), channel_id=1, source_target_pairs={{0,8},{4,12},{8,0},{12,4},{16,24},{20,28},{24,16},{28,20},{32,40},... | collective-permute-start | bytes 196616 | tf_op jit(solution)/shard_map/cond/branch_1_fun/ppermute | solution.py:17
  17.2 6.2 %conditional.38 = (bf16[128,256]{1,0:T(8,128)(2,1)S(1)}) conditional(s32[]{:T(128)} %bitcast.5, bf16[128,256]{1,0:T(8,128)(2,1)S(1)} %get-tuple-element.1022, bf16[128,256]{1,0:T(8,128)(2,1)S(1)} %get-tuple-element.1022), branch_computations={%region_4.0_spmd, %region_5.0_spmd} | conditional | bytes 393264 | solution.py:50
  19.6 3.8 %collective-permute-done.2 = bf16[128,256]{1,0:T(8,128)(2,1)S(1)} collective-permute-done((bf16[128,256]{1,0:T(8,128)(2,1)S(1)}, bf16[128,256]{1,0:T(8,128)(2,1)S(1)}, u32[]{:S(2)}, u32[]{:S(2)}) %collective-permute-start.2) | collective-permute-done | bytes 65568 | tf_op jit(solution)/shard_map/cond/branch_1_fun/ppermute | solution.py:17
  23.4 7.6 %conditional.39 = (bf16[128,256]{1,0:T(8,128)(2,1)S(1)}) conditional(s32[]{:T(128)} %bitcast.4, bf16[128,256]{1,0:T(8,128)(2,1)S(1)} %get-tuple-element.1023, bf16[128,256]{1,0:T(8,128)(2,1)S(1)} %get-tuple-element.1023), branch_computations={%region_6.0_spmd, %region_7.0_spmd} | conditional | bytes 393264 | solution.py:50
  25.6 5.4 %collective-permute-done.3 = bf16[128,256]{1,0:T(8,128)(2,1)S(1)} collective-permute-done((bf16[128,256]{1,0:T(8,128)(2,1)S(1)}, bf16[128,256]{1,0:T(8,128)(2,1)S(1)}, u32[]{:S(2)}, u32[]{:S(2)}) %collective-permute-start.3) | collective-permute-done | bytes 65568 | tf_op jit(solution)/shard_map/cond/branch_1_fun/ppermute | solution.py:17
  31.8 9.9 %all-to-all-start = ((bf16[4,128,256]{2,1,0:T(8,128)(2,1)}), bf16[4,128,256]{2,1,0:T(8,128)(2,1)S(1)}, u32[]{:S(2)}, u32[]{:S(2)}) async-start(bf16[4,128,256]{2,1,0:T(8,128)(2,1)} %broadcast_in_dim.51), calls=%async_computation | async-start | bytes 524288 | tf_op jit(solution)/shard_map/all_to_all | solution.py:22
  51.5 73.2 %while.34 = (s32[]{:T(128)}, f32[4,128,256]{2,0,1:T(4,128)S(1)}, f32[4,128,256]{2,0,1:T(4,128)S(1)}, s32[8,8]{1,0:T(8,128)S(1)}, bf16[4,128,256]{2,1,0:T(8,128)(...) while((s32[]{:T(128)}, f32[4,128,256]{2,0,1:T(4,128)S(1)}, ...), condition=%wide.region_15.17_spmd.clone.clone, body=%wide.region_14.16_spmd.clone.clone.sunk | while | flops 211192704 | bytes 13575092 | solution.py:126
  125.5 4.3 %all-to-all-start.1 = ((bf16[4,128,256]{2,1,0:T(8,128)(2,1)}), bf16[4,128,256]{2,1,0:T(8,128)(2,1)S(1)}, u32[]{:S(2)}, u32[]{:S(2)}) async-start(bf16[4,128,256]{2,1,0:T(8,128)(2,1)} %copy.66), calls=%async_computation.1 | async-start | bytes 524288 | tf_op jit(solution)/shard_map/all_to_all | solution.py:44
  130.2 8.8 %all-to-all-done.1 = bf16[4,128,256]{2,1,0:T(8,128)(2,1)S(1)} async-done(((bf16[4,128,256]{2,1,0:T(8,128)(2,1)}), bf16[4,128,256]{2,1,0:T(8,128)(2,1)S(1)}, u32[]{:S(2)}, u32[]{:S(2)}) %all-to-all-start.1) | async-done | bytes 262176 | tf_op jit(solution)/shard_map/all_to_all | solution.py:44
  142.3 6.2 %conditional.44 = (bf16[128,256]{1,0:T(8,128)(2,1)S(1)}) conditional(s32[]{:T(128)} %bitcast.6, bf16[128,256]{1,0:T(8,128)(2,1)S(1)} %get-tuple-element.1028, bf16[128,256]{1,0:T(8,128)(2,1)S(1)} %get-tuple-element.1028), branch_computations={%region_20.22_spmd, %region_21.23_spmd} | conditional | bytes 393264 | solution.py:50
  148.4 6.2 %conditional.45 = (bf16[128,256]{1,0:T(8,128)(2,1)S(1)}) conditional(s32[]{:T(128)} %bitcast.5, bf16[128,256]{1,0:T(8,128)(2,1)S(1)} %get-tuple-element.1029, bf16[128,256]{1,0:T(8,128)(2,1)S(1)} %get-tuple-element.1029), branch_computations={%region_22.24_spmd, %region_23.25_spmd} | conditional | bytes 393264 | solution.py:50
  150.3 4.2 %collective-permute-done.9 = bf16[128,256]{1,0:T(8,128)(2,1)S(1)} collective-permute-done((bf16[128,256]{1,0:T(8,128)(2,1)S(1)}, bf16[128,256]{1,0:T(8,128)(2,1)S(1)}, u32[]{:S(2)}, u32[]{:S(2)}) %collective-permute-start.9) | collective-permute-done | bytes 65568 | tf_op jit(solution)/shard_map/cond/branch_1_fun/ppermute | solution.py:17
  154.6 7.2 %conditional.46 = (bf16[128,256]{1,0:T(8,128)(2,1)S(1)}) conditional(s32[]{:T(128)} %bitcast.4, bf16[128,256]{1,0:T(8,128)(2,1)S(1)} %get-tuple-element.1030, bf16[128,256]{1,0:T(8,128)(2,1)S(1)} %get-tuple-element.1030), branch_computations={%region_24.26_spmd, %region_25.27_spmd} | conditional | bytes 393264 | solution.py:50
  156.5 5.3 %collective-permute-done.10 = bf16[128,256]{1,0:T(8,128)(2,1)S(1)} collective-permute-done((bf16[128,256]{1,0:T(8,128)(2,1)S(1)}, bf16[128,256]{1,0:T(8,128)(2,1)S(1)}, u32[]{:S(2)}, u32[]{:S(2)}) %collective-permute-start.10) | collective-permute-done | bytes 65568 | tf_op jit(solution)/shard_map/cond/branch_1_fun/ppermute | solution.py:17
  162.9 7.1 %conditional.53 = (bf16[128,256]{1,0:T(8,128)(2,1)S(1)}) conditional(s32[]{:T(128)} %bitcast.15, bf16[128,256]{1,0:T(8,128)(2,1)S(1)} %get-tuple-element.1036, bf16[128,256]{1,0:T(8,128)(2,1)S(1)} %get-tuple-element.1036), branch_computations={%region_40.42_spmd, %region_41.43_spmd} | conditional | bytes 393264 | solution.py:50
  164.8 5.1 %collective-permute-done.16 = bf16[128,256]{1,0:T(8,128)(2,1)S(1)} collective-permute-done((bf16[128,256]{1,0:T(8,128)(2,1)S(1)}, bf16[128,256]{1,0:T(8,128)(2,1)S(1)}, u32[]{:S(2)}, u32[]{:S(2)}) %collective-permute-start.16) | collective-permute-done | bytes 65568 | tf_op jit(solution)/shard_map/cond/branch_1_fun/ppermute | solution.py:17
  169.9 6.2 %conditional.55 = (bf16[128,256]{1,0:T(8,128)(2,1)S(1)}) conditional(s32[]{:T(128)} %bitcast.13, bf16[128,256]{1,0:T(8,128)(2,1)S(1)} %get-tuple-element.1038, bf16[128,256]{1,0:T(8,128)(2,1)S(1)} %get-tuple-element.1038), branch_computations={%region_44.46_spmd, %region_45.47_spmd} | conditional | bytes 393264 | solution.py:50
  180.6 9.3 %all-to-all-done.2 = bf16[4,128,256]{2,1,0:T(8,128)(2,1)S(1)} async-done(((bf16[4,128,256]{2,1,0:T(8,128)(2,1)}), bf16[4,128,256]{2,1,0:T(8,128)(2,1)S(1)}, u32[]{:S(2)}, u32[]{:S(2)}) %all-to-all-start.2) | async-done | bytes 262176 | tf_op jit(solution)/shard_map/all_to_all | solution.py:22
  189.9 45.1 %while.35 = (s32[]{:T(128)}, f32[4,128,256]{2,0,1:T(4,128)S(1)}, f32[4,128,256]{2,0,1:T(4,128)S(1)}, s32[8,8]{1,0:T(8,128)S(1)}, bf16[4,128,256]{2,1,0:T(8,128)(...) while((s32[]{:T(128)}, f32[4,128,256]{2,0,1:T(4,128)S(1)}, ...), condition=%wide.region_49.51_spmd.clone.clone, body=%wide.region_48.50_spmd.clone.clone.sunk | while | flops 211192704 | bytes 11477912 | solution.py:126
  241.8 6.5 %all-to-all-done.3 = bf16[4,128,256]{2,1,0:T(8,128)(2,1)S(1)} async-done(((bf16[4,128,256]{2,1,0:T(8,128)(2,1)}), bf16[4,128,256]{2,1,0:T(8,128)(2,1)S(1)}, u32[]{:S(2)}, u32[]{:S(2)}) %all-to-all-start.3) | async-done | bytes 262176 | tf_op jit(solution)/shard_map/all_to_all | solution.py:44
  248.5 7.1 %conditional.60 = (bf16[128,256]{1,0:T(8,128)(2,1)S(1)}) conditional(s32[]{:T(128)} %bitcast.15, bf16[128,256]{1,0:T(8,128)(2,1)S(1)} %get-tuple-element.1043, bf16[128,256]{1,0:T(8,128)(2,1)S(1)} %get-tuple-element.1043), branch_computations={%region_58.60_spmd, %region_59.61_spmd} | conditional | bytes 393264 | solution.py:50
  250.4 5.1 %collective-permute-done.23 = bf16[128,256]{1,0:T(8,128)(2,1)S(1)} collective-permute-done((bf16[128,256]{1,0:T(8,128)(2,1)S(1)}, bf16[128,256]{1,0:T(8,128)(2,1)S(1)}, u32[]{:S(2)}, u32[]{:S(2)}) %collective-permute-start.23) | collective-permute-done | bytes 65568 | tf_op jit(solution)/shard_map/cond/branch_1_fun/ppermute | solution.py:17
  255.6 6.2 %conditional.62 = (bf16[128,256]{1,0:T(8,128)(2,1)S(1)}) conditional(s32[]{:T(128)} %bitcast.13, bf16[128,256]{1,0:T(8,128)(2,1)S(1)} %get-tuple-element.1045, bf16[128,256]{1,0:T(8,128)(2,1)S(1)} %get-tuple-element.1045), branch_computations={%region_62.64_spmd, %region_63.65_spmd} | conditional | bytes 393264 | solution.py:50
  (449 shorter events, 185.5 us)
Async XLA Ops:
  7.4 3.1 %collective-permute-start = (bf16[128,256]{1,0:T(8,128)(2,1)S(1)}, bf16[128,256]{1,0:T(8,128)(2,1)S(1)}, u32[]{:S(2)}, u32[]{:S(2)}) collective-permute-start(bf16[128,256]{1,0:T(8,128)(2,1)S(1)} %param.1), channel_id=1, source_target_pairs={{0,4},{4,0},{8,12},{12,8},{16,20},{20,16},{24,28},{28,24},{32,36},... | collective-permute-start | bytes 196616 | tf_op jit(solution)/shard_map/cond/branch_1_fun/ppermute | solution.py:17
  10.5 6.7 %collective-permute-start.1 = (bf16[128,256]{1,0:T(8,128)(2,1)S(1)}, bf16[128,256]{1,0:T(8,128)(2,1)S(1)}, u32[]{:S(2)}, u32[]{:S(2)}) collective-permute-start(bf16[128,256]{1,0:T(8,128)(2,1)S(1)} %param.3), channel_id=1, source_target_pairs={{0,8},{4,12},{8,0},{12,4},{16,24},{20,28},{24,16},{28,20},{32,40},... | collective-permute-start | bytes 196616 | tf_op jit(solution)/shard_map/cond/branch_1_fun/ppermute | solution.py:17
  17.2 6.1 %collective-permute-start.2 = (bf16[128,256]{1,0:T(8,128)(2,1)S(1)}, bf16[128,256]{1,0:T(8,128)(2,1)S(1)}, u32[]{:S(2)}, u32[]{:S(2)}) collective-permute-start(bf16[128,256]{1,0:T(8,128)(2,1)S(1)} %param.5), channel_id=1, source_target_pairs={{0,16},{4,20},{8,24},{12,28},{16,0},{20,4},{24,8},{28,12},{32,48},... | collective-permute-start | bytes 196616 | tf_op jit(solution)/shard_map/cond/branch_1_fun/ppermute | solution.py:17
  23.4 7.6 %collective-permute-start.3 = (bf16[128,256]{1,0:T(8,128)(2,1)S(1)}, bf16[128,256]{1,0:T(8,128)(2,1)S(1)}, u32[]{:S(2)}, u32[]{:S(2)}) collective-permute-start(bf16[128,256]{1,0:T(8,128)(2,1)S(1)} %param.7), channel_id=1, source_target_pairs={{0,32},{4,36},{8,40},{12,44},{16,48},{20,52},{24,56},{28,60},{32,0... | collective-permute-start | bytes 196616 | tf_op jit(solution)/shard_map/cond/branch_1_fun/ppermute | solution.py:17
  31.0 16.1 %copy-start.1 = (f32[512,256]{1,0:T(8,128)S(1)}, f32[512,256]{1,0:T(8,128)}, u32[]{:S(2)}) copy-start(f32[512,256]{1,0:T(8,128)} %param.71) | copy-start | bytes 1572868
  31.8 15.3 %copy-start.7 = (f32[64,256]{1,0:T(8,128)S(1)}, f32[64,256]{1,0:T(8,128)}, u32[]{:S(2)}) copy-start(f32[64,256]{1,0:T(8,128)} %param.75) | copy-start | bytes 196612
  31.8 19.8 %all-to-all-start = ((bf16[4,128,256]{2,1,0:T(8,128)(2,1)}), bf16[4,128,256]{2,1,0:T(8,128)(2,1)S(1)}, u32[]{:S(2)}, u32[]{:S(2)}) async-start(bf16[4,128,256]{2,1,0:T(8,128)(2,1)} %broadcast_in_dim.51), calls=%async_computation | async-start | bytes 524288 | tf_op jit(solution)/shard_map/all_to_all | solution.py:22
  41.7 4.6 %copy-start.11 = (s32[1,1,2,64]{3,2,1,0:T(2,128)S(1)}, s32[1,1,2,64]{3,2,1,0:T(2,128)}, u32[]{:S(2)}) copy-start(s32[1,1,2,64]{3,2,1,0:T(2,128)} %param.77) | copy-start | bytes 1540
  63.6 2.3 copy-start
  72.7 2.2 copy-start
  125.5 13.6 %all-to-all-start.1 = ((bf16[4,128,256]{2,1,0:T(8,128)(2,1)}), bf16[4,128,256]{2,1,0:T(8,128)(2,1)S(1)}, u32[]{:S(2)}, u32[]{:S(2)}) async-start(bf16[4,128,256]{2,1,0:T(8,128)(2,1)} %copy.66), calls=%async_computation.1 | async-start | bytes 524288 | tf_op jit(solution)/shard_map/all_to_all | solution.py:44
  130.2 50.2 %copy-start.4 = (f32[4,128,256]{2,1,0:T(8,128)}, f32[4,128,256]{2,1,0:T(8,128)S(1)}, u32[]{:S(2)}) copy-start(f32[4,128,256]{2,1,0:T(8,128)S(1)} %copy.45) | copy-start | bytes 1572868
  139.1 3.1 %collective-permute-start.7 = (bf16[128,256]{1,0:T(8,128)(2,1)S(1)}, bf16[128,256]{1,0:T(8,128)(2,1)S(1)}, u32[]{:S(2)}, u32[]{:S(2)}) collective-permute-start(bf16[128,256]{1,0:T(8,128)(2,1)S(1)} %param.19), channel_id=1, source_target_pairs={{0,4},{4,0},{8,12},{12,8},{16,20},{20,16},{24,28},{28,24},{32,36},... | collective-permute-start | bytes 196616 | tf_op jit(solution)/shard_map/cond/branch_1_fun/ppermute | solution.py:17
  142.3 6.1 %collective-permute-start.8 = (bf16[128,256]{1,0:T(8,128)(2,1)S(1)}, bf16[128,256]{1,0:T(8,128)(2,1)S(1)}, u32[]{:S(2)}, u32[]{:S(2)}) collective-permute-start(bf16[128,256]{1,0:T(8,128)(2,1)S(1)} %param.21), channel_id=1, source_target_pairs={{0,8},{4,12},{8,0},{12,4},{16,24},{20,28},{24,16},{28,20},{32,40},... | collective-permute-start | bytes 196616 | tf_op jit(solution)/shard_map/cond/branch_1_fun/ppermute | solution.py:17
  148.4 6.1 %collective-permute-start.9 = (bf16[128,256]{1,0:T(8,128)(2,1)S(1)}, bf16[128,256]{1,0:T(8,128)(2,1)S(1)}, u32[]{:S(2)}, u32[]{:S(2)}) collective-permute-start(bf16[128,256]{1,0:T(8,128)(2,1)S(1)} %param.23), channel_id=1, source_target_pairs={{0,16},{4,20},{8,24},{12,28},{16,0},{20,4},{24,8},{28,12},{32,48},... | collective-permute-start | bytes 196616 | tf_op jit(solution)/shard_map/cond/branch_1_fun/ppermute | solution.py:17
  154.6 7.2 %collective-permute-start.10 = (bf16[128,256]{1,0:T(8,128)(2,1)S(1)}, bf16[128,256]{1,0:T(8,128)(2,1)S(1)}, u32[]{:S(2)}, u32[]{:S(2)}) collective-permute-start(bf16[128,256]{1,0:T(8,128)(2,1)S(1)} %param.25), channel_id=1, source_target_pairs={{0,32},{4,36},{8,40},{12,44},{16,48},{20,52},{24,56},{28,60},{32,0... | collective-permute-start | bytes 196616 | tf_op jit(solution)/shard_map/cond/branch_1_fun/ppermute | solution.py:17
  162.9 7.1 %collective-permute-start.16 = (bf16[128,256]{1,0:T(8,128)(2,1)S(1)}, bf16[128,256]{1,0:T(8,128)(2,1)S(1)}, u32[]{:S(2)}, u32[]{:S(2)}) collective-permute-start(bf16[128,256]{1,0:T(8,128)(2,1)S(1)} %param.39), channel_id=1, source_target_pairs={{0,32},{4,36},{8,40},{12,44},{16,48},{20,52},{24,56},{28,60},{32,0... | collective-permute-start | bytes 196616 | tf_op jit(solution)/shard_map/cond/branch_1_fun/ppermute | solution.py:17
  170.0 6.2 %collective-permute-start.18 = (bf16[128,256]{1,0:T(8,128)(2,1)S(1)}, bf16[128,256]{1,0:T(8,128)(2,1)S(1)}, u32[]{:S(2)}, u32[]{:S(2)}) collective-permute-start(bf16[128,256]{1,0:T(8,128)(2,1)S(1)} %param.43), channel_id=1, source_target_pairs={{0,128},{4,132},{8,136},{12,140},{16,144},{20,148},{24,152},{28,15... | collective-permute-start | bytes 196616 | tf_op jit(solution)/shard_map/cond/branch_1_fun/ppermute | solution.py:17
  176.1 4.3 %copy-start.2 = (f32[512,256]{1,0:T(8,128)S(1)}, f32[512,256]{1,0:T(8,128)}, u32[]{:S(2)}) copy-start(f32[512,256]{1,0:T(8,128)} %param.71) | copy-start | bytes 1572868
  176.9 3.5 %copy-start.8 = (f32[512]{0:T(512)S(1)}, f32[512]{0:T(512)}, u32[]{:S(2)}) copy-start(f32[512]{0:T(512)} %param.72) | copy-start | bytes 6148
  176.9 13.0 %all-to-all-start.2 = ((bf16[4,128,256]{2,1,0:T(8,128)(2,1)}), bf16[4,128,256]{2,1,0:T(8,128)(2,1)S(1)}, u32[]{:S(2)}, u32[]{:S(2)}) async-start(bf16[4,128,256]{2,1,0:T(8,128)(2,1)} %broadcast_in_dim.58), calls=%async_computation.2 | async-start | bytes 524288 | tf_op jit(solution)/shard_map/all_to_all | solution.py:22
  235.9 12.5 %all-to-all-start.3 = ((bf16[4,128,256]{2,1,0:T(8,128)(2,1)}), bf16[4,128,256]{2,1,0:T(8,128)(2,1)S(1)}, u32[]{:S(2)}, u32[]{:S(2)}) async-start(bf16[4,128,256]{2,1,0:T(8,128)(2,1)} %copy.65), calls=%async_computation.3 | async-start | bytes 524288 | tf_op jit(solution)/shard_map/all_to_all | solution.py:44
  248.5 7.1 %collective-permute-start.23 = (bf16[128,256]{1,0:T(8,128)(2,1)S(1)}, bf16[128,256]{1,0:T(8,128)(2,1)S(1)}, u32[]{:S(2)}, u32[]{:S(2)}) collective-permute-start(bf16[128,256]{1,0:T(8,128)(2,1)S(1)} %param.55), channel_id=1, source_target_pairs={{0,32},{4,36},{8,40},{12,44},{16,48},{20,52},{24,56},{28,60},{32,0... | collective-permute-start | bytes 196616 | tf_op jit(solution)/shard_map/cond/branch_1_fun/ppermute | solution.py:17
  255.6 6.2 %collective-permute-start.25 = (bf16[128,256]{1,0:T(8,128)(2,1)S(1)}, bf16[128,256]{1,0:T(8,128)(2,1)S(1)}, u32[]{:S(2)}, u32[]{:S(2)}) collective-permute-start(bf16[128,256]{1,0:T(8,128)(2,1)S(1)} %param.59), channel_id=1, source_target_pairs={{0,128},{4,132},{8,136},{12,140},{16,144},{20,148},{24,152},{28,15... | collective-permute-start | bytes 196616 | tf_op jit(solution)/shard_map/cond/branch_1_fun/ppermute | solution.py:17
  (44 other events, 51.9 us)
where the time goes:
time: 265 us; the launch traced here: 263 us
  waiting for transfers between devices  71.2 us (27%)
  matrix products  67 us (25%)
  starting transfers between devices  50.1 us (19%)
  local copies, waits for them, and re-layouts  46.8 us (18%)
  other arithmetic  15.9 us (6%)
  between operations  10.1 us (4%)
    ppermute x12, waiting for transfers between devices, partner(): lax.ppermute(array, axis, [(i, i ^ 1 << bit) for i in range(lax.axis_size...  43.6 us
    ppermute x12, starting transfers between devices, partner(): lax.ppermute(array, axis, [(i, i ^ 1 << bit) for i in range(lax.axis_size...  29 us
    dot_general x16, matrix products, group_step(): dst_total = dst_total + jnp.einsum('ts,tnd->snd', dst_onehot, dst_terms)  19.6 us
    gather x16, local copies, waits for them, and re-layouts, group_step(): src_pick = jnp.take(src_blocks, src_index, axis=0)  15.6 us
    dot_general x16, matrix products, group_step(): jnp.einsum('tnd,tmd->tnm', src_rel, dst_pick, preferred_element_type=jnp....  15.4 us
    all_to_all x2, waiting for transfers between devices, sum_at_owner(): lax.all_to_all(cut_along(array, dim, length), axis, 0, 0, tiled=True)  15.4 us
    while x80, local copies, waits for them, and re-layouts  13.5 us
    all_to_all x2, starting transfers between devices, from_everyone(): return lax.all_to_all(copies, axis, split_axis=0, concat_axis=0, tiled=True)  13.4 us
  transfers between devices with their start and end apart: 16, of which 16 were waited for; matrix products, arithmetic and copies ran while one was open for 1% of the time, Pallas kernels for 0%

commit v1 on v0

--- a/solution.py
+++ b/solution.py
@@ -1,13 +1,13 @@
 import jax
 import jax.numpy as jnp
 from jax import lax
+from jax.experimental import pallas as pl
+from jax.experimental.pallas import tpu as pltpu
 from jax.sharding import PartitionSpec as P
 
 D = 256
 TILE = 128
-TILE_GROUP = 8
 ROUNDS = 2
-MAXT = 64
 
 
 learn_rate = 0.1
@@ -70,63 +70,59 @@
     return rows
 
 
-def tile_work(src_rows, partition, tile_list, rel_list, live_count, rel_table):
-    dst_number = partition.shape[0] // TILE
-    src_number = src_rows.shape[0] // TILE
-    rel_number = rel_table.shape[0]
-    score_scale = D ** (-0.5)
-    src_blocks = src_rows.reshape(src_number, TILE, D)
-    dst_blocks = partition.reshape(dst_number, TILE, D)
-    group_count = MAXT // TILE_GROUP
-    tile_grid = tile_list.reshape(group_count, TILE_GROUP)
-    rel_grid = rel_list.reshape(group_count, TILE_GROUP)
-    slot_grid = jnp.arange(MAXT, dtype=jnp.int32).reshape(group_count, TILE_GROUP)
-    diagonal_ones = jnp.eye(TILE, dtype=jnp.float32)
-    src_range = jnp.arange(src_number, dtype=jnp.int32)
-    dst_range = jnp.arange(dst_number, dtype=jnp.int32)
-    rel_range = jnp.arange(rel_number, dtype=jnp.int32)
+UNROLL = 4
 
-    def group_step(totals, group_item):
-        src_total, dst_total = totals
-        tile_ids, rel_ids, slot_ids = group_item
-        src_index = tile_ids // dst_number
-        dst_index = tile_ids % dst_number
-        rel_onehot = (rel_ids[:, None] == rel_range[None, :]).astype(jnp.float32)
-        rel_pick = jnp.dot(rel_onehot, rel_table)
-        src_pick = jnp.take(src_blocks, src_index, axis=0)
-        dst_pick = jnp.take(dst_blocks, dst_index, axis=0)
-        src_rel = (src_pick * rel_pick[:, None, :]).astype(jnp.bfloat16)
-        scores = (
-            jnp.einsum("tnd,tmd->tnm", src_rel, dst_pick, preferred_element_type=jnp.float32)
-            * score_scale
-        )
-        live_tiles = (slot_ids < live_count).astype(jnp.float32)
-        slope = ((jax.nn.sigmoid(scores) - diagonal_ones) * live_tiles[:, None, None]).astype(
-            jnp.bfloat16
-        )
-        src_terms = (
-            jnp.einsum("tnm,tmd->tnd", slope, dst_pick, preferred_element_type=jnp.float32)
-            * rel_pick[:, None, :]
-            * score_scale
-        )
-        dst_terms = (
-            jnp.einsum("tnm,tnd->tmd", slope, src_rel, preferred_element_type=jnp.float32)
-            * score_scale
-        )
-        src_onehot = (src_index[:, None] == src_range[None, :]).astype(jnp.float32)
-        dst_onehot = (dst_index[:, None] == dst_range[None, :]).astype(jnp.float32)
-        src_total = src_total + jnp.einsum("ts,tnd->snd", src_onehot, src_terms)
-        dst_total = dst_total + jnp.einsum("ts,tnd->snd", dst_onehot, dst_terms)
-        return ((src_total, dst_total), None)
 
-    start_totals = (
-        jnp.zeros((src_number, TILE, D), jnp.float32),
-        jnp.zeros((dst_number, TILE, D), jnp.float32),
-    )
-    (src_total, dst_total), unused = lax.scan(
-        group_step, start_totals, (tile_grid, rel_grid, slot_grid)
-    )
-    return (src_total.reshape(-1, D), dst_total.reshape(-1, D))
+def tile_kernel(code_ref, rel_id_ref, count_ref, src_ref, part_ref, rel_ref, src_out, dst_out, src_low):
+    src_low[...] = src_ref[...].astype(jnp.bfloat16).astype(jnp.float32)
+    src_out[...] = jnp.zeros_like(src_out)
+    dst_out[...] = jnp.zeros_like(dst_out)
+    live = count_ref[0]
+    row = lax.broadcasted_iota(jnp.int32, (TILE, TILE), 0)
+    col = lax.broadcasted_iota(jnp.int32, (TILE, TILE), 1)
+    shift = jnp.where(row == col, -0.5, 0.5).astype(jnp.float32)
+
+    def step(group, carry):
+        for lane in range(UNROLL):
+            slot = group * UNROLL + lane
+            code = code_ref[slot]
+            s = pl.multiple_of((code // 4) * TILE, TILE)
+            e = pl.multiple_of((code % 4) * TILE, TILE)
+            rel = rel_ref[pl.ds(rel_id_ref[slot], 1), :]
+            src_rel = (src_low[pl.ds(s, TILE), :] * rel).astype(jnp.bfloat16)
+            dst = part_ref[pl.ds(e, TILE), :]
+            scores = lax.dot_general(
+                src_rel, dst, (((1,), (1,)), ((), ())), preferred_element_type=jnp.float32
+            )
+            on = jnp.where(slot < live, 1.0, 0.0).astype(jnp.float32)
+            slope = ((jnp.tanh(scores * (0.5 * D**-0.5)) * 0.5 + shift) * on).astype(jnp.bfloat16)
+            src_term = jnp.dot(slope, dst, preferred_element_type=jnp.float32)
+            dst_term = lax.dot_general(
+                slope, src_rel, (((0,), (0,)), ((), ())), preferred_element_type=jnp.float32
+            )
+            src_out[pl.ds(s, TILE), :] += src_term * rel
+            dst_out[pl.ds(e, TILE), :] += dst_term
+        return carry
+
+    lax.fori_loop(0, (live + UNROLL - 1) // UNROLL, step, 0)
+    src_out[...] = src_out[...] * D**-0.5
+    dst_out[...] = dst_out[...] * D**-0.5
+
+
+def tile_work(src_table, partition, tile_list, rel_list, live_count, rel_table):
+    smem = pl.BlockSpec(memory_space=pltpu.SMEM)
+    vmem = pl.BlockSpec(memory_space=pltpu.VMEM)
+    return pl.pallas_call(
+        tile_kernel,
+        out_shape=(
+            jax.ShapeDtypeStruct(src_table.shape, jnp.float32),
+            jax.ShapeDtypeStruct(partition.shape, jnp.float32),
+        ),
+        in_specs=[smem, smem, smem, vmem, vmem, vmem],
+        out_specs=(vmem, vmem),
+        scratch_shapes=[pltpu.VMEM(src_table.shape, jnp.float32)],
+        compiler_params=pltpu.CompilerParams(vmem_limit_bytes=32 * 2**20),
+    )(tile_list, rel_list, live_count, src_table, partition, rel_table)
 
 
 def adagrad(embedding, accumulator, gradient):
@@ -145,11 +141,11 @@
         moved_rows = route_slice(own_rows, round_mask, bit_count)
         partition = gather_directly(moved_rows, "rep", 0)
         src_grad, dst_part = tile_work(
-            src_table.astype(jnp.bfloat16),
+            src_table,
             partition,
             tiles[0, 0, round_index],
             tile_rel[0, 0, round_index],
-            counts[0, 0, round_index],
+            counts[0, 0, round_index : round_index + 1],
             rel_table,
         )
         summed = sum_at_owner(dst_part.astype(jnp.bfloat16), "rep", 0).astype(jnp.bfloat16)

time: 265 us -> 169 us (0.64)
  the two profiles are of different devices: /device:TPU:30 before, /device:TPU:62 now
where the time goes in v1:
time: 169 us; the launch traced here: 168 us
  waiting for transfers between devices  65.3 us (39%)
  starting transfers between devices  53.1 us (31%)
  Pallas kernels  28.7 us (17%)
  between operations  9.9 us (6%)
  other arithmetic  5.99 us (4%)
  local copies, waits for them, and re-layouts  4.24 us (3%)
    ppermute x12, waiting for transfers between devices, partner(): lax.ppermute(array, axis, [(i, i ^ 1 << bit) for i in range(lax.axis_size...  34.2 us
    ppermute x12, starting transfers between devices, partner(): lax.ppermute(array, axis, [(i, i ^ 1 << bit) for i in range(lax.axis_size...  33.1 us
    pallas_call x2, Pallas kernels, tile_work(): pl.pallas_call(tile_kernel, out_shape=(jax.ShapeDtypeStruct(src_table.sha...  28.7 us
    all_to_all x2, waiting for transfers between devices, from_everyone(): return lax.all_to_all(copies, axis, split_axis=0, concat_axis=0, tiled=True)  19.2 us
    all_to_all x2, starting transfers between devices, from_everyone(): return lax.all_to_all(copies, axis, split_axis=0, concat_axis=0, tiled=True)  13.3 us
    all_to_all x2, waiting for transfers between devices, sum_at_owner(): lax.all_to_all(cut_along(array, dim, length), axis, 0, 0, tiled=True)  11.9 us
    all_to_all x2, starting transfers between devices, sum_at_owner(): lax.all_to_all(cut_along(array, dim, length), axis, 0, 0, tiled=True)  6.82 us
  transfers between devices with their start and end apart: 16, of which 16 were waited for; matrix products, arithmetic and copies ran while one was open for 1% of the time, Pallas kernels for 0%

profile of v1, /device:TPU:62, one launch (start us, length us, event | category | flops | bytes accessed | tf_op | source)
XLA Modules:
  0.0 167.6 jit_solution(561431017007610200)
XLA Ops:
  10.5 6.7 %conditional.37 = (bf16[128,256]{1,0:T(8,128)(2,1)S(1)}) conditional(s32[]{:T(128)} %bitcast.8, bf16[128,256]{1,0:T(8,128)(2,1)S(1)} %get-tuple-element.204, bf16[128,256]{1,0:T(8,128)(2,1)S(1)} %get-tuple-element.204), branch_computations={%region_2.0_spmd, %region_3.0_spmd} | conditional | bytes 393264 | solution.py:50
  10.5 4.3 %collective-permute-start.1 = (bf16[128,256]{1,0:T(8,128)(2,1)S(1)}, bf16[128,256]{1,0:T(8,128)(2,1)S(1)}, u32[]{:S(2)}, u32[]{:S(2)}) collective-permute-start(bf16[128,256]{1,0:T(8,128)(2,1)S(1)} %param.3), channel_id=1, source_target_pairs={{0,8},{4,12},{8,0},{12,4},{16,24},{20,28},{24,16},{28,20},{32,40},... | collective-permute-start | bytes 196616 | tf_op jit(solution)/shard_map/cond/branch_1_fun/ppermute | solution.py:17
  17.2 7.2 %conditional.39 = (bf16[128,256]{1,0:T(8,128)(2,1)S(1)}) conditional(s32[]{:T(128)} %bitcast.6, bf16[128,256]{1,0:T(8,128)(2,1)S(1)} %get-tuple-element.206, bf16[128,256]{1,0:T(8,128)(2,1)S(1)} %get-tuple-element.206), branch_computations={%region_6.0_spmd, %region_7.0_spmd} | conditional | bytes 393264 | solution.py:50
  17.2 4.0 %collective-permute-start.3 = (bf16[128,256]{1,0:T(8,128)(2,1)S(1)}, bf16[128,256]{1,0:T(8,128)(2,1)S(1)}, u32[]{:S(2)}, u32[]{:S(2)}) collective-permute-start(bf16[128,256]{1,0:T(8,128)(2,1)S(1)} %param.7), channel_id=1, source_target_pairs={{0,32},{4,36},{8,40},{12,44},{16,48},{20,52},{24,56},{28,60},{32,0... | collective-permute-start | bytes 196616 | tf_op jit(solution)/shard_map/cond/branch_1_fun/ppermute | solution.py:17
  25.2 9.7 %all-to-all-start = ((bf16[4,128,256]{2,1,0:T(8,128)(2,1)}), bf16[4,128,256]{2,1,0:T(8,128)(2,1)S(1)}, u32[]{:S(2)}, u32[]{:S(2)}) async-start(bf16[4,128,256]{2,1,0:T(8,128)(2,1)} %broadcast_in_dim.4), calls=%async_computation | async-start | bytes 524288 | tf_op jit(solution)/shard_map/all_to_all | solution.py:22
  35.7 9.4 %all-to-all-done = bf16[4,128,256]{2,1,0:T(8,128)(2,1)S(1)} async-done(((bf16[4,128,256]{2,1,0:T(8,128)(2,1)}), bf16[4,128,256]{2,1,0:T(8,128)(2,1)S(1)}, u32[]{:S(2)}, u32[]{:S(2)}) %all-to-all-start) | async-done | bytes 262176 | tf_op jit(solution)/shard_map/all_to_all | solution.py:22
  45.0 14.3 %shard_map.120 = (f32[512,256]{1,0:T(8,128)S(1)}, f32[512,256]{1,0:T(8,128)S(1)}) custom-call(s32[64]{0:T(128)S(1)} %get-tuple-element.194.code_ref, s32[64]{0:T(128)S(1)} %get-tuple-element.189.rel_id_ref, s32[1]{0:T(128)} %bitcast.2.count_ref, f32[512,256]{1,0:T(8,128)S(1)} %copy-done, bf16[512,256]{1,0:T(8,128)(2,1)S(1)} %bitcast.29, f32[64,256]{1,0:T(8,128)S(1)} %copy-done.1), custom_call_target="tpu_custom_call" | custom-call | tf_op jit(solution)/shard_map/pallas_call | solution.py:115
  60.1 3.4 %all-to-all-start.1 = ((bf16[4,128,256]{2,1,0:T(8,128)(2,1)}), bf16[4,128,256]{2,1,0:T(8,128)(2,1)S(1)}, u32[]{:S(2)}, u32[]{:S(2)}) async-start(bf16[4,128,256]{2,1,0:T(8,128)(2,1)} %bitcast.21), calls=%async_computation.1 | async-start | bytes 524288 | tf_op jit(solution)/shard_map/all_to_all | solution.py:44
  68.2 4.4 %all-to-all-done.1 = bf16[4,128,256]{2,1,0:T(8,128)(2,1)S(1)} async-done(((bf16[4,128,256]{2,1,0:T(8,128)(2,1)}), bf16[4,128,256]{2,1,0:T(8,128)(2,1)S(1)}, u32[]{:S(2)}, u32[]{:S(2)}) %all-to-all-start.1) | async-done | bytes 262176 | tf_op jit(solution)/shard_map/all_to_all | solution.py:44
  75.8 6.2 %conditional.44 = (bf16[128,256]{1,0:T(8,128)(2,1)S(1)}) conditional(s32[]{:T(128)} %bitcast.8, bf16[128,256]{1,0:T(8,128)(2,1)S(1)} %get-tuple-element.211, bf16[128,256]{1,0:T(8,128)(2,1)S(1)} %get-tuple-element.211), branch_computations={%region_18.0_spmd, %region_19.0_spmd} | conditional | bytes 393264 | solution.py:50
  81.9 7.1 %conditional.46 = (bf16[128,256]{1,0:T(8,128)(2,1)S(1)}) conditional(s32[]{:T(128)} %bitcast.6, bf16[128,256]{1,0:T(8,128)(2,1)S(1)} %get-tuple-element.213, bf16[128,256]{1,0:T(8,128)(2,1)S(1)} %get-tuple-element.213), branch_computations={%region_22.0_spmd, %region_23.0_spmd} | conditional | bytes 393264 | solution.py:50
  81.9 4.2 %collective-permute-start.10 = (bf16[128,256]{1,0:T(8,128)(2,1)S(1)}, bf16[128,256]{1,0:T(8,128)(2,1)S(1)}, u32[]{:S(2)}, u32[]{:S(2)}) collective-permute-start(bf16[128,256]{1,0:T(8,128)(2,1)S(1)} %param.21), channel_id=1, source_target_pairs={{0,32},{4,36},{8,40},{12,44},{16,48},{20,52},{24,56},{28,60},{32,0... | collective-permute-start | bytes 196616 | tf_op jit(solution)/shard_map/cond/branch_1_fun/ppermute | solution.py:17
  93.2 6.2 %conditional.52 = (bf16[128,256]{1,0:T(8,128)(2,1)S(1)}) conditional(s32[]{:T(128)} %bitcast.18, bf16[128,256]{1,0:T(8,128)(2,1)S(1)} %get-tuple-element.218, bf16[128,256]{1,0:T(8,128)(2,1)S(1)} %get-tuple-element.218), branch_computations={%region_36.0_spmd, %region_37.0_spmd} | conditional | bytes 393264 | solution.py:50
  99.4 7.7 %conditional.56 = (bf16[128,256]{1,0:T(8,128)(2,1)S(1)}) conditional(s32[]{:T(128)} %bitcast.14, bf16[128,256]{1,0:T(8,128)(2,1)S(1)} %get-tuple-element.222, bf16[128,256]{1,0:T(8,128)(2,1)S(1)} %get-tuple-element.222), branch_computations={%region_44.0_spmd, %region_45.0_spmd} | conditional | bytes 393264 | solution.py:50
  102.3 4.8 %collective-permute-done.19 = bf16[128,256]{1,0:T(8,128)(2,1)S(1)} collective-permute-done((bf16[128,256]{1,0:T(8,128)(2,1)S(1)}, bf16[128,256]{1,0:T(8,128)(2,1)S(1)}, u32[]{:S(2)}, u32[]{:S(2)}) %collective-permute-start.19) | collective-permute-done | bytes 65568 | tf_op jit(solution)/shard_map/cond/branch_1_fun/ppermute | solution.py:17
  107.8 3.5 %all-to-all-start.2 = ((bf16[4,128,256]{2,1,0:T(8,128)(2,1)}), bf16[4,128,256]{2,1,0:T(8,128)(2,1)S(1)}, u32[]{:S(2)}, u32[]{:S(2)}) async-start(bf16[4,128,256]{2,1,0:T(8,128)(2,1)} %broadcast_in_dim.5), calls=%async_computation.2 | async-start | bytes 524288 | tf_op jit(solution)/shard_map/all_to_all | solution.py:22
  111.5 9.9 %all-to-all-done.2 = bf16[4,128,256]{2,1,0:T(8,128)(2,1)S(1)} async-done(((bf16[4,128,256]{2,1,0:T(8,128)(2,1)}), bf16[4,128,256]{2,1,0:T(8,128)(2,1)S(1)}, u32[]{:S(2)}, u32[]{:S(2)}) %all-to-all-start.2) | async-done | bytes 262176 | tf_op jit(solution)/shard_map/all_to_all | solution.py:22
  121.4 14.4 %shard_map.121 = (f32[512,256]{1,0:T(8,128)S(1)}, f32[512,256]{1,0:T(8,128)S(1)}) custom-call(s32[64]{0:T(128)S(1)} %get-tuple-element.195.code_ref, s32[64]{0:T(128)S(1)} %get-tuple-element.188.rel_id_ref, s32[1]{0:T(128)} %bitcast.13.count_ref, f32[512,256]{1,0:T(8,128)S(1)} %divide_subtract_fusion.1.src_ref, bf16[512,256]{1,0:T(8,128)(2,1)S(1)} %bitcast.28, ...), custom_call_target="tpu_custom_call" | custom-call | tf_op jit(solution)/shard_map/pallas_call | solution.py:115
  136.6 3.4 %all-to-all-start.3 = ((bf16[4,128,256]{2,1,0:T(8,128)(2,1)}), bf16[4,128,256]{2,1,0:T(8,128)(2,1)S(1)}, u32[]{:S(2)}, u32[]{:S(2)}) async-start(bf16[4,128,256]{2,1,0:T(8,128)(2,1)} %bitcast.23), calls=%async_computation.3 | async-start | bytes 524288 | tf_op jit(solution)/shard_map/all_to_all | solution.py:44
  141.6 7.5 %all-to-all-done.3 = bf16[4,128,256]{2,1,0:T(8,128)(2,1)S(1)} async-done(((bf16[4,128,256]{2,1,0:T(8,128)(2,1)}), bf16[4,128,256]{2,1,0:T(8,128)(2,1)S(1)}, u32[]{:S(2)}, u32[]{:S(2)}) %all-to-all-start.3) | async-done | bytes 262176 | tf_op jit(solution)/shard_map/all_to_all | solution.py:44
  152.3 6.2 %conditional.59 = (bf16[128,256]{1,0:T(8,128)(2,1)S(1)}) conditional(s32[]{:T(128)} %bitcast.18, bf16[128,256]{1,0:T(8,128)(2,1)S(1)} %get-tuple-element.225, bf16[128,256]{1,0:T(8,128)(2,1)S(1)} %get-tuple-element.225), branch_computations={%region_52.0_spmd, %region_53.0_spmd} | conditional | bytes 393264 | solution.py:50
  154.2 4.2 %collective-permute-done.22 = bf16[128,256]{1,0:T(8,128)(2,1)S(1)} collective-permute-done((bf16[128,256]{1,0:T(8,128)(2,1)S(1)}, bf16[128,256]{1,0:T(8,128)(2,1)S(1)}, u32[]{:S(2)}, u32[]{:S(2)}) %collective-permute-start.22) | collective-permute-done | bytes 65568 | tf_op jit(solution)/shard_map/cond/branch_1_fun/ppermute | solution.py:17
  158.5 7.8 %conditional.65 = (bf16[128,256]{1,0:T(8,128)(2,1)S(1)}, f32[128]{0:T(128)S(1)}) conditional(s32[]{:T(128)} %bitcast.14, bf16[128,256]{1,0:T(8,128)(2,1)S(1)} %get-tuple-element.229, bf16[128,256]{1,0:T(8,128)(2,1)S(1)} %get-tuple-element.229), branch_computations={%region_60.62_spmd, %region_62.64_spmd} | conditional | flops 98176 | bytes 459320
  160.5 5.7 %collective-permute-done.27 = bf16[128,256]{1,0:T(8,128)(2,1)S(1)} collective-permute-done((bf16[128,256]{1,0:T(8,128)(2,1)S(1)}, bf16[128,256]{1,0:T(8,128)(2,1)S(1)}, u32[]{:S(2)}, u32[]{:S(2)}) %collective-permute-start.27) | collective-permute-done | bytes 65568 | tf_op jit(solution)/shard_map/cond/branch_1_fun/ppermute | solution.py:17
  (88 shorter events, 63.1 us)
Async XLA Ops:
  7.4 3.1 %collective-permute-start = (bf16[128,256]{1,0:T(8,128)(2,1)S(1)}, bf16[128,256]{1,0:T(8,128)(2,1)S(1)}, u32[]{:S(2)}, u32[]{:S(2)}) collective-permute-start(bf16[128,256]{1,0:T(8,128)(2,1)S(1)} %param.1), channel_id=1, source_target_pairs={{0,4},{4,0},{8,12},{12,8},{16,20},{20,16},{24,28},{28,24},{32,36},... | collective-permute-start | bytes 196616 | tf_op jit(solution)/shard_map/cond/branch_1_fun/ppermute | solution.py:17
  10.5 6.7 %collective-permute-start.1 = (bf16[128,256]{1,0:T(8,128)(2,1)S(1)}, bf16[128,256]{1,0:T(8,128)(2,1)S(1)}, u32[]{:S(2)}, u32[]{:S(2)}) collective-permute-start(bf16[128,256]{1,0:T(8,128)(2,1)S(1)} %param.3), channel_id=1, source_target_pairs={{0,8},{4,12},{8,0},{12,4},{16,24},{20,28},{24,16},{28,20},{32,40},... | collective-permute-start | bytes 196616 | tf_op jit(solution)/shard_map/cond/branch_1_fun/ppermute | solution.py:17
  17.2 7.2 %collective-permute-start.3 = (bf16[128,256]{1,0:T(8,128)(2,1)S(1)}, bf16[128,256]{1,0:T(8,128)(2,1)S(1)}, u32[]{:S(2)}, u32[]{:S(2)}) collective-permute-start(bf16[128,256]{1,0:T(8,128)(2,1)S(1)} %param.7), channel_id=1, source_target_pairs={{0,32},{4,36},{8,40},{12,44},{16,48},{20,52},{24,56},{28,60},{32,0... | collective-permute-start | bytes 196616 | tf_op jit(solution)/shard_map/cond/branch_1_fun/ppermute | solution.py:17
  24.5 20.6 %copy-start = (f32[512,256]{1,0:T(8,128)S(1)}, f32[512,256]{1,0:T(8,128)}, u32[]{:S(2)}) copy-start(f32[512,256]{1,0:T(8,128)} %src_ref.1) | copy-start | bytes 1572868
  25.2 9.7 %copy-start.4 = (s32[1,1,2]{2,1,0:T(1,128)S(1)}, s32[1,1,2]{2,1,0:T(1,128)}, u32[]{:S(2)}) copy-start(s32[1,1,2]{2,1,0:T(1,128)} %param.73) | copy-start | bytes 28
  25.2 19.8 %copy-start.1 = (f32[64,256]{1,0:T(8,128)S(1)}, f32[64,256]{1,0:T(8,128)}, u32[]{:S(2)}) copy-start(f32[64,256]{1,0:T(8,128)} %rel_ref.3) | copy-start | bytes 196612
  25.2 19.8 %all-to-all-start = ((bf16[4,128,256]{2,1,0:T(8,128)(2,1)}), bf16[4,128,256]{2,1,0:T(8,128)(2,1)S(1)}, u32[]{:S(2)}, u32[]{:S(2)}) async-start(bf16[4,128,256]{2,1,0:T(8,128)(2,1)} %broadcast_in_dim.4), calls=%async_computation | async-start | bytes 524288 | tf_op jit(solution)/shard_map/all_to_all | solution.py:22
  35.0 0.7 copy-start.5
  35.0 0.7 copy-start.6
  60.1 12.5 %all-to-all-start.1 = ((bf16[4,128,256]{2,1,0:T(8,128)(2,1)}), bf16[4,128,256]{2,1,0:T(8,128)(2,1)S(1)}, u32[]{:S(2)}, u32[]{:S(2)}) async-start(bf16[4,128,256]{2,1,0:T(8,128)(2,1)} %bitcast.21), calls=%async_computation.1 | async-start | bytes 524288 | tf_op jit(solution)/shard_map/all_to_all | solution.py:44
  72.6 3.1 %collective-permute-start.7 = (bf16[128,256]{1,0:T(8,128)(2,1)S(1)}, bf16[128,256]{1,0:T(8,128)(2,1)S(1)}, u32[]{:S(2)}, u32[]{:S(2)}) collective-permute-start(bf16[128,256]{1,0:T(8,128)(2,1)S(1)} %param.15), channel_id=1, source_target_pairs={{0,4},{4,0},{8,12},{12,8},{16,20},{20,16},{24,28},{28,24},{32,36},... | collective-permute-start | bytes 196616 | tf_op jit(solution)/shard_map/cond/branch_1_fun/ppermute | solution.py:17
  75.8 6.1 %collective-permute-start.8 = (bf16[128,256]{1,0:T(8,128)(2,1)S(1)}, bf16[128,256]{1,0:T(8,128)(2,1)S(1)}, u32[]{:S(2)}, u32[]{:S(2)}) collective-permute-start(bf16[128,256]{1,0:T(8,128)(2,1)S(1)} %param.17), channel_id=1, source_target_pairs={{0,8},{4,12},{8,0},{12,4},{16,24},{20,28},{24,16},{28,20},{32,40},... | collective-permute-start | bytes 196616 | tf_op jit(solution)/shard_map/cond/branch_1_fun/ppermute | solution.py:17
  81.9 7.1 %collective-permute-start.10 = (bf16[128,256]{1,0:T(8,128)(2,1)S(1)}, bf16[128,256]{1,0:T(8,128)(2,1)S(1)}, u32[]{:S(2)}, u32[]{:S(2)}) collective-permute-start(bf16[128,256]{1,0:T(8,128)(2,1)S(1)} %param.21), channel_id=1, source_target_pairs={{0,32},{4,36},{8,40},{12,44},{16,48},{20,52},{24,56},{28,60},{32,0... | collective-permute-start | bytes 196616 | tf_op jit(solution)/shard_map/cond/branch_1_fun/ppermute | solution.py:17
  89.0 0.9 copy-start.2
  89.1 0.7 copy-start.7
  90.0 3.1 %collective-permute-start.13 = (bf16[128,256]{1,0:T(8,128)(2,1)S(1)}, bf16[128,256]{1,0:T(8,128)(2,1)S(1)}, u32[]{:S(2)}, u32[]{:S(2)}) collective-permute-start(bf16[128,256]{1,0:T(8,128)(2,1)S(1)} %param.29), channel_id=1, source_target_pairs={{0,4},{4,0},{8,12},{12,8},{16,20},{20,16},{24,28},{28,24},{32,36},... | collective-permute-start | bytes 196616 | tf_op jit(solution)/shard_map/cond/branch_1_fun/ppermute | solution.py:17
  93.2 6.2 %collective-permute-start.15 = (bf16[128,256]{1,0:T(8,128)(2,1)S(1)}, bf16[128,256]{1,0:T(8,128)(2,1)S(1)}, u32[]{:S(2)}, u32[]{:S(2)}) collective-permute-start(bf16[128,256]{1,0:T(8,128)(2,1)S(1)} %param.33), channel_id=1, source_target_pairs={{0,16},{4,20},{8,24},{12,28},{16,0},{20,4},{24,8},{28,12},{32,48},... | collective-permute-start | bytes 196616 | tf_op jit(solution)/shard_map/cond/branch_1_fun/ppermute | solution.py:17
  99.4 7.7 %collective-permute-start.19 = (bf16[128,256]{1,0:T(8,128)(2,1)S(1)}, bf16[128,256]{1,0:T(8,128)(2,1)S(1)}, u32[]{:S(2)}, u32[]{:S(2)}) collective-permute-start(bf16[128,256]{1,0:T(8,128)(2,1)S(1)} %param.41), channel_id=1, source_target_pairs={{0,256},{4,260},{8,264},{12,268},{16,272},{20,276},{24,280},{28,28... | collective-permute-start | bytes 196616 | tf_op jit(solution)/shard_map/cond/branch_1_fun/ppermute | solution.py:17
  107.8 3.6 %copy-start.3 = (f32[512]{0:T(512)S(1)}, f32[512]{0:T(512)}, u32[]{:S(2)}) copy-start(f32[512]{0:T(512)} %param.66) | copy-start | bytes 6148
  107.8 13.6 %all-to-all-start.2 = ((bf16[4,128,256]{2,1,0:T(8,128)(2,1)}), bf16[4,128,256]{2,1,0:T(8,128)(2,1)S(1)}, u32[]{:S(2)}, u32[]{:S(2)}) async-start(bf16[4,128,256]{2,1,0:T(8,128)(2,1)} %broadcast_in_dim.5), calls=%async_computation.2 | async-start | bytes 524288 | tf_op jit(solution)/shard_map/all_to_all | solution.py:22
  136.6 12.5 %all-to-all-start.3 = ((bf16[4,128,256]{2,1,0:T(8,128)(2,1)}), bf16[4,128,256]{2,1,0:T(8,128)(2,1)S(1)}, u32[]{:S(2)}, u32[]{:S(2)}) async-start(bf16[4,128,256]{2,1,0:T(8,128)(2,1)} %bitcast.23), calls=%async_computation.3 | async-start | bytes 524288 | tf_op jit(solution)/shard_map/all_to_all | solution.py:44
  149.1 3.1 %collective-permute-start.20 = (bf16[128,256]{1,0:T(8,128)(2,1)S(1)}, bf16[128,256]{1,0:T(8,128)(2,1)S(1)}, u32[]{:S(2)}, u32[]{:S(2)}) collective-permute-start(bf16[128,256]{1,0:T(8,128)(2,1)S(1)} %param.43), channel_id=1, source_target_pairs={{0,4},{4,0},{8,12},{12,8},{16,20},{20,16},{24,28},{28,24},{32,36},... | collective-permute-start | bytes 196616 | tf_op jit(solution)/shard_map/cond/branch_1_fun/ppermute | solution.py:17
  152.3 6.2 %collective-permute-start.22 = (bf16[128,256]{1,0:T(8,128)(2,1)S(1)}, bf16[128,256]{1,0:T(8,128)(2,1)S(1)}, u32[]{:S(2)}, u32[]{:S(2)}) collective-permute-start(bf16[128,256]{1,0:T(8,128)(2,1)S(1)} %param.47), channel_id=1, source_target_pairs={{0,16},{4,20},{8,24},{12,28},{16,0},{20,4},{24,8},{28,12},{32,48},... | collective-permute-start | bytes 196616 | tf_op jit(solution)/shard_map/cond/branch_1_fun/ppermute | solution.py:17
  158.5 7.7 %collective-permute-start.27 = (bf16[128,256]{1,0:T(8,128)(2,1)S(1)}, bf16[128,256]{1,0:T(8,128)(2,1)S(1)}, u32[]{:S(2)}, u32[]{:S(2)}) collective-permute-start(bf16[128,256]{1,0:T(8,128)(2,1)S(1)} %param.55), channel_id=1, source_target_pairs={{0,256},{4,260},{8,264},{12,268},{16,272},{20,276},{24,280},{28,28... | collective-permute-start | bytes 196616 | tf_op jit(solution)/shard_map/cond/branch_1_fun/ppermute | solution.py:17
